TPU v7x, 1024 devices: a whole 8x8x8 slice. The times are simulated.
1024 devices in a mesh: node: 128 (over y, x, core), local: 8 (over z).
Axes of the slice: x: 8, y: 8, z: 8, core: 2. Of those that a mesh axis runs over, the one named last changes fastest.
Arguments:
- expert_ids: int32 [4096, 8], P('node'), may hold values from 0 to 255, as said below
- slot_gates: float32 [128, 2, 256], P('node'), may hold values from 0 to 0.6, as said below
- expert_rows: bfloat16 [128, 256, 2, 7168], P('node', None, None, 'local'), may hold values from -6 to 6
- residual: bfloat16 [4096, 7168], P('node', 'local')
- norm_gain: float32 [7168], P('local'), may hold values from 0.25 to 1.75
- w_q_down: bfloat16 [7168, 1536], P('local'), may hold values from -0.0625 to 0.0625
- w_kv_down: bfloat16 [7168, 576], P('local'), may hold values from -0.0625 to 0.0625
Outputs:
- hidden: bfloat16 [4096, 7168], P('node', 'local')
- q_latent: bfloat16 [4096, 1536], P(('node', 'local'))
- kv_latent: bfloat16 [4096, 576], P(('node', 'local'))
Inputs may be any that keep to these rules, and one draw needn't show every extreme that they name: `expert_ids`: each token names both experts of each of 4 different nodes; expert e lives on node e // 2. Of the tokens of one node, at most 2 use any one node, and exactly 2 use some node. `slot_gates`: slot s * 2 + j of node m serves the j-th token, in order, of node s that uses node m; its weights are positive, and zero on slots that serve no token.
All inputs are finite; a program needn't handle non-finite values.
Results may differ from a plain program's by a relative error of at most 0.0058.
Values may be sent and summed in bfloat16 or wider, within the bound.
A program may use at most 32 MiB of HBM per device.

v0:
```python
import jax
import jax.numpy as jnp
from jax import lax
from jax.sharding import PartitionSpec as P

D = 7168
QL = 1536
EXP_NODE = 2


epsilon = 1e-06


def on_device(expert_ids, slot_gates, expert_rows, residual, norm_gain, w_q_down, w_kv_down):
    node_count = lax.axis_size("node")
    slot_total = expert_rows.shape[1]
    per_node = slot_total // node_count
    weighted = jnp.zeros((slot_total, expert_rows.shape[3]), jnp.float32)
    for expert in range(EXP_NODE):
        weighted = weighted + slot_gates[0, expert][:, None] * expert_rows[0, :, expert, :].astype(
            jnp.float32
        )
    node_part = weighted.astype(jnp.bfloat16)
    column_total = node_part.shape[1]
    node_ids = expert_ids // EXP_NODE
    routed = jnp.max(
        (node_ids[:, :, None] == lax.iota(jnp.int32, node_count)[None, None, :]).astype(jnp.int32),
        axis=1,
    )
    slot_rank = jnp.cumsum(routed, axis=0) - routed
    slot_hits = (slot_rank[:, :, None] == lax.iota(jnp.int32, per_node)[None, None, :]) & (
        routed[:, :, None] == 1
    )
    selector = slot_hits.astype(jnp.bfloat16).reshape(routed.shape[0], slot_total)
    block_width = min(128, column_total)
    combined_blocks = []
    for column_block in range(column_total // block_width):
        block_cols = node_part[:, column_block * block_width : (column_block + 1) * block_width]
        arrived_block = lax.all_to_all(block_cols, "node", split_axis=0, concat_axis=0, tiled=True)
        combined_blocks.append(jnp.dot(selector, arrived_block, preferred_element_type=jnp.float32))
    combined = jnp.concatenate(combined_blocks, axis=1)
    hidden = (residual.astype(jnp.float32) + combined).astype(jnp.bfloat16)
    hidden_f = hidden.astype(jnp.float32)
    square_sum = lax.psum(jnp.sum(hidden_f * hidden_f, axis=1), "local")
    normed = (hidden_f * lax.rsqrt(square_sum / D + epsilon)[:, None] * norm_gain).astype(
        jnp.bfloat16
    )
    query_part = jnp.dot(normed, w_q_down, preferred_element_type=jnp.float32)
    latent_part = jnp.dot(normed, w_kv_down, preferred_element_type=jnp.float32)
    latent = lax.psum_scatter(
        jnp.concatenate([query_part, latent_part], axis=1), "local", scatter_dimension=0, tiled=True
    )
    return (hidden, latent[:, :QL].astype(jnp.bfloat16), latent[:, QL:].astype(jnp.bfloat16))


def solution(mesh):
    return jax.shard_map(
        on_device,
        mesh=mesh,
        in_specs=(
            P("node", None),
            P("node", None, None),
            P("node", None, None, "local"),
            P("node", "local"),
            P("local"),
            P("local", None),
            P("local", None),
        ),
        out_specs=(P("node", "local"), P(("node", "local"), None), P(("node", "local"), None)),
        check_vma=False,
    )
```

profile of v0, /device:TPU:2, one launch (start us, length us, event | category | flops | bytes accessed | tf_op | source)
XLA Modules:
  0.0 197.0 jit_solution(3720029882412162155)
XLA Ops:
  0.6 0.0 copy-start
  0.6 0.0 copy-start.6
  0.7 0.0 copy-start.5
  0.7 3.2 %fusion.47 = (bf16[1,256,1,896]{3,2,1,0:T(2,128)(2,1)S(1)}, bf16[1,256,1,896]{3,2,1,0:T(2,128)(2,1)S(1)}) fusion(bf16[1,256,2,896]{3,2,1,0:T(2,128)(2,1)} %param.9), kind=kLoop, calls=%fused_computation.64 | loop fusion | bytes 1835008 | tf_op jit(solution)/shard_map/slice | solution.py:20
  3.9 0.0 copy-done.6
  3.9 0.0 copy-start.3
  3.9 0.0 copy-start.4
  3.9 0.2 fusion.8
  4.2 0.8 fusion.48
  5.0 18.3 %all-to-all-start = ((bf16[128,2,128]{2,1,0:T(2,128)(2,1)}), bf16[128,2,128]{2,1,0:T(2,128)(2,1)S(1)}, u32[]{:S(2)}, u32[]{:S(2)}) async-start(bf16[128,2,128]{2,1,0:T(2,128)(2,1)} %bitcast.4), calls=%async_computation | async-start | bytes 131072 | tf_op jit(solution)/shard_map/all_to_all | solution.py:39
  23.3 0.0 copy-done.5
  23.4 0.1 copy.32
  23.4 0.1 convert_reduce_fusion
  23.6 0.1 reduce_window_sum.11
  23.6 1.3 dynamic-slice
  25.6 8.6 %all-to-all-done = bf16[128,2,128]{2,1,0:T(2,128)(2,1)S(1)} async-done(((bf16[128,2,128]{2,1,0:T(2,128)(2,1)}), bf16[128,2,128]{2,1,0:T(2,128)(2,1)S(1)}, u32[]{:S(2)}, u32[]{:S(2)}) %all-to-all-start) | async-done | bytes 65568 | tf_op jit(solution)/shard_map/all_to_all | solution.py:39
  34.2 6.4 %all-to-all-start.1 = ((bf16[128,2,128]{2,1,0:T(2,128)(2,1)}), bf16[128,2,128]{2,1,0:T(2,128)(2,1)S(1)}, u32[]{:S(2)}, u32[]{:S(2)}) async-start(bf16[128,2,128]{2,1,0:T(2,128)(2,1)} %bitcast.6), calls=%async_computation.1 | async-start | bytes 131072 | tf_op jit(solution)/shard_map/all_to_all | solution.py:39
  40.6 0.1 fusion.6
  40.7 10.7 %all-to-all-done.1 = bf16[128,2,128]{2,1,0:T(2,128)(2,1)S(1)} async-done(((bf16[128,2,128]{2,1,0:T(2,128)(2,1)}), bf16[128,2,128]{2,1,0:T(2,128)(2,1)S(1)}, u32[]{:S(2)}, u32[]{:S(2)}) %all-to-all-start.1) | async-done | bytes 65568 | tf_op jit(solution)/shard_map/all_to_all | solution.py:39
  51.4 6.4 %all-to-all-start.2 = ((bf16[128,2,128]{2,1,0:T(2,128)(2,1)}), bf16[128,2,128]{2,1,0:T(2,128)(2,1)S(1)}, u32[]{:S(2)}, u32[]{:S(2)}) async-start(bf16[128,2,128]{2,1,0:T(2,128)(2,1)} %bitcast.8), calls=%async_computation.2 | async-start | bytes 131072 | tf_op jit(solution)/shard_map/all_to_all | solution.py:39
  57.8 0.1 fusion.5
  57.9 10.7 %all-to-all-done.2 = bf16[128,2,128]{2,1,0:T(2,128)(2,1)S(1)} async-done(((bf16[128,2,128]{2,1,0:T(2,128)(2,1)}), bf16[128,2,128]{2,1,0:T(2,128)(2,1)S(1)}, u32[]{:S(2)}, u32[]{:S(2)}) %all-to-all-start.2) | async-done | bytes 65568 | tf_op jit(solution)/shard_map/all_to_all | solution.py:39
  68.7 6.4 %all-to-all-start.3 = ((bf16[128,2,128]{2,1,0:T(2,128)(2,1)}), bf16[128,2,128]{2,1,0:T(2,128)(2,1)S(1)}, u32[]{:S(2)}, u32[]{:S(2)}) async-start(bf16[128,2,128]{2,1,0:T(2,128)(2,1)} %bitcast.10), calls=%async_computation.3 | async-start | bytes 131072 | tf_op jit(solution)/shard_map/all_to_all | solution.py:39
  75.0 0.1 fusion.4
  75.2 10.8 %all-to-all-done.3 = bf16[128,2,128]{2,1,0:T(2,128)(2,1)S(1)} async-done(((bf16[128,2,128]{2,1,0:T(2,128)(2,1)}), bf16[128,2,128]{2,1,0:T(2,128)(2,1)S(1)}, u32[]{:S(2)}, u32[]{:S(2)}) %all-to-all-start.3) | async-done | bytes 65568 | tf_op jit(solution)/shard_map/all_to_all | solution.py:39
  85.9 6.6 %all-to-all-start.4 = ((bf16[128,2,128]{2,1,0:T(2,128)(2,1)}), bf16[128,2,128]{2,1,0:T(2,128)(2,1)S(1)}, u32[]{:S(2)}, u32[]{:S(2)}) async-start(bf16[128,2,128]{2,1,0:T(2,128)(2,1)} %bitcast.12), calls=%async_computation.4 | async-start | bytes 131072 | tf_op jit(solution)/shard_map/all_to_all | solution.py:39
  92.5 0.1 fusion.3
  92.7 10.7 %all-to-all-done.4 = bf16[128,2,128]{2,1,0:T(2,128)(2,1)S(1)} async-done(((bf16[128,2,128]{2,1,0:T(2,128)(2,1)}), bf16[128,2,128]{2,1,0:T(2,128)(2,1)S(1)}, u32[]{:S(2)}, u32[]{:S(2)}) %all-to-all-start.4) | async-done | bytes 65568 | tf_op jit(solution)/shard_map/all_to_all | solution.py:39
  103.4 6.4 %all-to-all-start.5 = ((bf16[128,2,128]{2,1,0:T(2,128)(2,1)}), bf16[128,2,128]{2,1,0:T(2,128)(2,1)S(1)}, u32[]{:S(2)}, u32[]{:S(2)}) async-start(bf16[128,2,128]{2,1,0:T(2,128)(2,1)} %bitcast.14), calls=%async_computation.5 | async-start | bytes 131072 | tf_op jit(solution)/shard_map/all_to_all | solution.py:39
  109.8 0.1 fusion.2
  109.9 10.7 %all-to-all-done.5 = bf16[128,2,128]{2,1,0:T(2,128)(2,1)S(1)} async-done(((bf16[128,2,128]{2,1,0:T(2,128)(2,1)}), bf16[128,2,128]{2,1,0:T(2,128)(2,1)S(1)}, u32[]{:S(2)}, u32[]{:S(2)}) %all-to-all-start.5) | async-done | bytes 65568 | tf_op jit(solution)/shard_map/all_to_all | solution.py:39
  120.7 6.4 %all-to-all-start.6 = ((bf16[128,2,128]{2,1,0:T(2,128)(2,1)}), bf16[128,2,128]{2,1,0:T(2,128)(2,1)S(1)}, u32[]{:S(2)}, u32[]{:S(2)}) async-start(bf16[128,2,128]{2,1,0:T(2,128)(2,1)} %bitcast.16), calls=%async_computation.6 | async-start | bytes 131072 | tf_op jit(solution)/shard_map/all_to_all | solution.py:39
  127.0 0.1 fusion.1
  127.2 10.6 %all-to-all-done.6 = bf16[128,2,128]{2,1,0:T(2,128)(2,1)S(1)} async-done(((bf16[128,2,128]{2,1,0:T(2,128)(2,1)}), bf16[128,2,128]{2,1,0:T(2,128)(2,1)S(1)}, u32[]{:S(2)}, u32[]{:S(2)}) %all-to-all-start.6) | async-done | bytes 65568 | tf_op jit(solution)/shard_map/all_to_all | solution.py:39
  137.8 0.1 fusion
  137.9 0.0 copy-done.3
  137.9 0.1 fusion.9
  138.1 0.0 copy-start.2
  138.1 25.5 %psum.7 = f32[32]{0:T(128)S(1)} all-reduce(f32[32]{0:T(128)S(1)} %get-tuple-element.3), channel_id=1, replica_groups=mesh['node'=128,'local'=8] {'local'}, use_global_device_ids=true, to_apply=%region_3.4 | all-reduce | flops 32 | bytes 256 | tf_op jit(solution)/shard_map/psum | solution.py:44
  163.6 0.0 copy-done
  163.6 0.0 copy-done.4
  163.6 0.6 fusion.43
  164.2 0.6 copy-done.1
  164.8 0.4 fusion.41
  165.3 30.4 %all-reduce.2 = bf16[32,2112]{1,0:T(8,128)(2,1)S(1)} all-reduce(f32[32,2112]{1,0:T(8,128)S(1)} %pad_maximum_fusion), channel_id=2, replica_groups=mesh['node'=128,'local'=8] {'local'}, use_global_device_ids=true, to_apply=%region_4.5.clone | all-reduce | flops 67584 | bytes 405504
  195.8 0.6 slice.61
  196.4 0.6 slice.62
  197.0 0.0 copy-done.2
  (8 shorter events, 0.1 us)
Async XLA Ops:
  0.6 163.0 %copy-start = (bf16[896,1536]{1,0:T(8,128)(2,1)S(1)}, bf16[896,1536]{1,0:T(8,128)(2,1)}, u32[]{:S(2)}) copy-start(bf16[896,1536]{1,0:T(8,128)(2,1)} %param.12) | copy-start | bytes 8257540
  0.6 3.2 %copy-start.6 = (f32[1,2,256]{2,1,0:T(2,128)S(1)}, f32[1,2,256]{2,1,0:T(2,128)}, u32[]{:S(2)}) copy-start(f32[1,2,256]{2,1,0:T(2,128)} %param.8) | copy-start | bytes 6148
  0.7 22.7 %copy-start.5 = (s32[32,8]{0,1:T(8,128)S(1)}, s32[32,8]{0,1:T(8,128)}, u32[]{:S(2)}) copy-start(s32[32,8]{0,1:T(8,128)} %param.7) | copy-start | bytes 3076
  3.9 134.0 %copy-start.3 = (bf16[32,896]{1,0:T(8,128)(2,1)S(1)}, bf16[32,896]{1,0:T(8,128)(2,1)}, u32[]{:S(2)}) copy-start(bf16[32,896]{1,0:T(8,128)(2,1)} %param.10) | copy-start | bytes 172036
  3.9 159.7 %copy-start.4 = (f32[896]{0:T(1024)S(1)}, f32[896]{0:T(1024)}, u32[]{:S(2)}) copy-start(f32[896]{0:T(1024)} %param.11) | copy-start | bytes 10756
  5.0 29.2 %all-to-all-start = ((bf16[128,2,128]{2,1,0:T(2,128)(2,1)}), bf16[128,2,128]{2,1,0:T(2,128)(2,1)S(1)}, u32[]{:S(2)}, u32[]{:S(2)}) async-start(bf16[128,2,128]{2,1,0:T(2,128)(2,1)} %bitcast.4), calls=%async_computation | async-start | bytes 131072 | tf_op jit(solution)/shard_map/all_to_all | solution.py:39
  34.2 17.2 %all-to-all-start.1 = ((bf16[128,2,128]{2,1,0:T(2,128)(2,1)}), bf16[128,2,128]{2,1,0:T(2,128)(2,1)S(1)}, u32[]{:S(2)}, u32[]{:S(2)}) async-start(bf16[128,2,128]{2,1,0:T(2,128)(2,1)} %bitcast.6), calls=%async_computation.1 | async-start | bytes 131072 | tf_op jit(solution)/shard_map/all_to_all | solution.py:39
  51.4 17.3 %all-to-all-start.2 = ((bf16[128,2,128]{2,1,0:T(2,128)(2,1)}), bf16[128,2,128]{2,1,0:T(2,128)(2,1)S(1)}, u32[]{:S(2)}, u32[]{:S(2)}) async-start(bf16[128,2,128]{2,1,0:T(2,128)(2,1)} %bitcast.8), calls=%async_computation.2 | async-start | bytes 131072 | tf_op jit(solution)/shard_map/all_to_all | solution.py:39
  68.7 17.3 %all-to-all-start.3 = ((bf16[128,2,128]{2,1,0:T(2,128)(2,1)}), bf16[128,2,128]{2,1,0:T(2,128)(2,1)S(1)}, u32[]{:S(2)}, u32[]{:S(2)}) async-start(bf16[128,2,128]{2,1,0:T(2,128)(2,1)} %bitcast.10), calls=%async_computation.3 | async-start | bytes 131072 | tf_op jit(solution)/shard_map/all_to_all | solution.py:39
  85.9 17.5 %all-to-all-start.4 = ((bf16[128,2,128]{2,1,0:T(2,128)(2,1)}), bf16[128,2,128]{2,1,0:T(2,128)(2,1)S(1)}, u32[]{:S(2)}, u32[]{:S(2)}) async-start(bf16[128,2,128]{2,1,0:T(2,128)(2,1)} %bitcast.12), calls=%async_computation.4 | async-start | bytes 131072 | tf_op jit(solution)/shard_map/all_to_all | solution.py:39
  103.4 17.2 %all-to-all-start.5 = ((bf16[128,2,128]{2,1,0:T(2,128)(2,1)}), bf16[128,2,128]{2,1,0:T(2,128)(2,1)S(1)}, u32[]{:S(2)}, u32[]{:S(2)}) async-start(bf16[128,2,128]{2,1,0:T(2,128)(2,1)} %bitcast.14), calls=%async_computation.5 | async-start | bytes 131072 | tf_op jit(solution)/shard_map/all_to_all | solution.py:39
  120.7 17.2 %all-to-all-start.6 = ((bf16[128,2,128]{2,1,0:T(2,128)(2,1)}), bf16[128,2,128]{2,1,0:T(2,128)(2,1)S(1)}, u32[]{:S(2)}, u32[]{:S(2)}) async-start(bf16[128,2,128]{2,1,0:T(2,128)(2,1)} %bitcast.16), calls=%async_computation.6 | async-start | bytes 131072 | tf_op jit(solution)/shard_map/all_to_all | solution.py:39
  138.1 58.9 %copy-start.2 = (bf16[32,896]{1,0:T(8,128)(2,1)}, bf16[32,896]{1,0:T(8,128)(2,1)S(1)}, u32[]{:S(2)}) copy-start(bf16[32,896]{1,0:T(8,128)(2,1)S(1)} %get-tuple-element.4) | copy-start | bytes 172036
  163.6 1.2 copy-start.1
where the time goes:
time: 198 us; the launch traced here: 197 us
  waiting for transfers between devices  72.9 us (37%)
  starting transfers between devices  56.8 us (29%)
  blocking collectives  56 us (28%)
  local copies, waits for them, and re-layouts  7.24 us (4%)
    all_to_all x7, waiting for transfers between devices, on_device(): lax.all_to_all(block_cols, 'node', split_axis=0, concat_axis=0, tiled=True)  72.9 us
    all_to_all x7, starting transfers between devices, on_device(): lax.all_to_all(block_cols, 'node', split_axis=0, concat_axis=0, tiled=True)  56.8 us
    unnamed x1, blocking collectives  30.4 us
    psum x1, blocking collectives, on_device(): square_sum = lax.psum(jnp.sum(hidden_f * hidden_f, axis=1), 'local')  25.5 us
  transfers between devices with their start and end apart: 7, of which 7 were waited for; matrix products, arithmetic and copies ran while one was open for 1% of the time, Pallas kernels for 0%

commit v1 on v0

v1 whole, which is shorter than its diff:
```python
import jax
import jax.numpy as jnp
from jax import lax
from jax.experimental import pallas as pl
from jax.experimental.pallas import tpu as pltpu
from jax.sharding import PartitionSpec as P

D = 7168
QL = 1536
KVL = 576
TOK = 32
OWN = 4
NODES = 128
SLOTS = 256
COLS = 896
BLOCKS = COLS // 128
LAT_BLOCKS = 17
LOCALS = 8
HI_LANE = 64
LO_LANE = 96
EPSILON = 1e-06
f32, bf16 = jnp.float32, jnp.bfloat16
MESH = pl.DeviceIdType.MESH


def partner(me, k):
    dx, dy, dc = k & 7, (k + (k >> 3)) & 7, k >> 6
    y, x, c = me >> 4, (me >> 1) & 7, me & 1
    return (((y + dy) & 7) << 4) | (((x + dx) & 7) << 1) | ((c + dc) & 1)


def wait_bytes(ref, sem):
    pltpu.make_async_copy(ref, ref, sem).wait()


def kernel(
    ids_hbm, gates_hbm, rows_hbm, res_hbm, gain_hbm, wq_hbm, wkv_hbm,
    hid_out, q_out, kv_out,
    ids, gates, rows, res, gain, wq, wkv, send, recv, scaled, zsend, zrecv,
    in_sem, send_sem, recv_sem, zsend_sem, zrecv_sem,
):
    me = lax.axis_index("node")
    z = lax.axis_index("local")
    loads = [
        pltpu.make_async_copy(source, target, in_sem.at[i])
        for i, (source, target) in enumerate(
            [
                (gates_hbm.at[0], gates), (rows_hbm.at[0], rows), (ids_hbm, ids), (res_hbm, res),
                (gain_hbm, gain), (wq_hbm, wq), (wkv_hbm, wkv),
            ]
        )
    ]
    for load in loads:
        load.start()

    barrier = pltpu.get_barrier_semaphore()

    def greet(k, carry):
        pl.semaphore_signal(
            barrier, inc=1, device_id={"node": partner(me, k)}, device_id_type=MESH
        )
        return carry

    lax.fori_loop(1, NODES, greet, 0)
    for k in range(1, LOCALS):
        pl.semaphore_signal(barrier, inc=1, device_id={"local": (z + k) & 7}, device_id_type=MESH)

    loads[0].wait()
    gate_columns = jnp.concatenate([gates[...], jnp.zeros((6, SLOTS), f32)], axis=0).T
    loads[1].wait()
    pairs = rows[...].astype(f32)
    weighted = pairs[:, 0, :] * gate_columns[:, 0:1] + pairs[:, 1, :] * gate_columns[:, 1:2]
    send_rows = send.reshape(BLOCKS, SLOTS, 128)
    for block in range(BLOCKS):
        send_rows[block] = weighted[:, 128 * block : 128 * block + 128].astype(bf16)

    pl.semaphore_wait(barrier, NODES - 1 + LOCALS - 1)

    def push(k, carry):
        other = partner(me, k)
        pltpu.make_async_remote_copy(
            src_ref=send.at[:, other], dst_ref=recv.at[:, me], send_sem=send_sem, recv_sem=recv_sem,
            device_id={"node": other}, device_id_type=MESH,
        ).start()
        return carry

    lax.fori_loop(1, NODES, push, 0)
    pltpu.make_async_copy(send.at[:, me], recv.at[:, me], recv_sem).start()

    for load in loads[2:5]:
        load.wait()
    slot = lax.broadcasted_iota(jnp.int32, (SLOTS, TOK), 0)
    nodes = ids[...] >> 1
    routed = nodes[0:1, :] == (slot >> 1)
    for entry in range(1, 8):
        routed = routed | (nodes[entry : entry + 1, :] == (slot >> 1))
    earlier = (
        lax.broadcasted_iota(jnp.int32, (TOK, TOK), 0)
        < lax.broadcasted_iota(jnp.int32, (TOK, TOK), 1)
    ).astype(bf16)
    rank = jnp.dot(routed.astype(bf16), earlier, preferred_element_type=f32)
    serves = (routed & (rank == (slot & 1).astype(f32))).astype(bf16)

    wait_bytes(recv, recv_sem)
    recv_rows = recv.reshape(BLOCKS, SLOTS, 128)
    squares = jnp.zeros((TOK, 128), f32)
    for block in range(BLOCKS):
        cols = slice(128 * block, 128 * block + 128)
        combined = lax.dot_general(
            serves, recv_rows[block], (((0,), (0,)), ((), ())), preferred_element_type=f32
        )
        hidden = (res[:, cols].astype(f32) + combined).astype(bf16)
        hid_out[:, cols] = hidden
        hidden = hidden.astype(f32)
        squares = squares + hidden * hidden
        scaled[:, cols] = (hidden * gain[:, cols]).astype(bf16)

    loads[5].wait()
    loads[6].wait()
    zsend_rows = zsend.reshape(LAT_BLOCKS, TOK, 128)
    stream = scaled[...]
    query = jnp.dot(stream, wq[...], preferred_element_type=f32)
    for block in range(12):
        zsend_rows[block] = query[:, 128 * block : 128 * block + 128].astype(bf16)
    keys = lax.dot_general(stream, wkv[...], (((1,), (1,)), ((), ())), preferred_element_type=f32)
    for block in range(4):
        zsend_rows[12 + block] = keys[:, 128 * block : 128 * block + 128].astype(bf16)
    quarter = jnp.sum(squares, axis=1, keepdims=True) * 0.25
    high = quarter.astype(bf16)
    low = jnp.where(quarter < jnp.inf, quarter - high.astype(f32), 0.0).astype(bf16)
    zsend_rows[16] = jnp.concatenate(
        [
            keys[:, 512:576].astype(bf16),
            jnp.broadcast_to(high, (TOK, LO_LANE - HI_LANE)),
            jnp.broadcast_to(low, (TOK, 128 - LO_LANE)),
        ],
        axis=1,
    )
    for k in range(1, LOCALS):
        other = (z + k) & 7
        pltpu.make_async_remote_copy(
            src_ref=zsend.at[:, other], dst_ref=zrecv.at[z], send_sem=zsend_sem, recv_sem=zrecv_sem,
            device_id={"local": other}, device_id_type=MESH,
        ).start()
    pltpu.make_async_copy(zsend.at[:, z], zrecv.at[z], zrecv_sem).start()
    wait_bytes(send.at[:, pl.ds(0, NODES - 1)], send_sem)
    wait_bytes(zrecv, zrecv_sem)

    zrecv_rows = zrecv.reshape(LOCALS, LAT_BLOCKS * OWN, 128)
    total = zrecv_rows[0].astype(f32)
    for source in range(1, LOCALS):
        total = total + zrecv_rows[source].astype(f32)
    last = total[16 * OWN : 17 * OWN]
    square_sum = (last[:, HI_LANE : HI_LANE + 1] + last[:, LO_LANE : LO_LANE + 1]) * 4.0
    finite = square_sum < jnp.inf
    inverse = lax.rsqrt(square_sum / D + EPSILON)
    for block in range(LAT_BLOCKS):
        part = total[OWN * block : OWN * block + OWN]
        part = jnp.where(finite, part * inverse, 0.0).astype(bf16)
        if block < 12:
            q_out[:, 128 * block : 128 * block + 128] = part
        elif block < 16:
            kv_out[:, 128 * block - QL : 128 * block - QL + 128] = part
        else:
            kv_out[:, 512:576] = part[:, 0:64]
    wait_bytes(zrecv.at[pl.ds(0, LOCALS - 1)], zsend_sem)


def on_device(expert_ids, slot_gates, expert_rows, residual, norm_gain, w_q_down, w_kv_down):
    anywhere = pl.BlockSpec(memory_space=pl.ANY)
    vmem = pl.BlockSpec(memory_space=pltpu.VMEM)
    return pl.pallas_call(
        kernel,
        out_shape=(
            jax.ShapeDtypeStruct((TOK, COLS), bf16),
            jax.ShapeDtypeStruct((OWN, QL), bf16),
            jax.ShapeDtypeStruct((OWN, KVL), bf16),
        ),
        in_specs=[anywhere] * 7,
        out_specs=(vmem,) * 3,
        scratch_shapes=[
            pltpu.VMEM((8, TOK), jnp.int32),
            pltpu.VMEM((2, SLOTS), f32),
            pltpu.VMEM((SLOTS, 2, COLS), bf16),
            pltpu.VMEM((TOK, COLS), bf16),
            pltpu.VMEM((1, COLS), f32),
            pltpu.VMEM((COLS, QL), bf16),
            pltpu.VMEM((KVL, COLS), bf16),
            pltpu.VMEM((BLOCKS, NODES, 2, 128), bf16),
            pltpu.VMEM((BLOCKS, NODES, 2, 128), bf16),
            pltpu.VMEM((TOK, COLS), bf16),
            pltpu.VMEM((LAT_BLOCKS, LOCALS, OWN, 128), bf16),
            pltpu.VMEM((LOCALS, LAT_BLOCKS, OWN, 128), bf16),
            pltpu.SemaphoreType.DMA((7,)),
            pltpu.SemaphoreType.DMA,
            pltpu.SemaphoreType.DMA,
            pltpu.SemaphoreType.DMA,
            pltpu.SemaphoreType.DMA,
        ],
        compiler_params=pltpu.CompilerParams(
            collective_id=0, has_side_effects=True, vmem_limit_bytes=56 * 1024 * 1024
        ),
        name="combine_norm_project",
    )(
        expert_ids.T, slot_gates, expert_rows, residual, norm_gain.reshape(1, COLS), w_q_down,
        w_kv_down.T,
    )


def solution(mesh):
    return jax.shard_map(
        on_device,
        mesh=mesh,
        in_specs=(
            P("node", None),
            P("node", None, None),
            P("node", None, None, "local"),
            P("node", "local"),
            P("local"),
            P("local", None),
            P("local", None),
        ),
        out_specs=(P("node", "local"), P(("node", "local"), None), P(("node", "local"), None)),
        check_vma=False,
    )
```

time: 198 us -> 54.3 us (0.27)
  the two profiles are of different devices: /device:TPU:2 before, /device:TPU:1 now
where the time goes in v1:
time: 54.3 us; the launch traced here: 54 us
  Pallas kernels  48.1 us (89%)
  local copies, waits for them, and re-layouts  5.31 us (10%)
  between operations  0.64 us (1%)
    pallas_call x1, Pallas kernels, on_device(): pl.pallas_call(kernel, out_shape=(jax.ShapeDtypeStruct((TOK, COLS), bf16)...  48.1 us
    unnamed x3, local copies, waits for them, and re-layouts  4.04 us
    reshape x1, local copies, waits for them, and re-layouts, on_device(): norm_gain.reshape(1, COLS)  1.27 us

profile of v1, /device:TPU:1, one launch (start us, length us, event | category | flops | bytes accessed | tf_op | source)
XLA Modules:
  0.0 54.0 jit_solution(15825203596824985100)
XLA Ops:
  0.6 1.3 %reshape.9.gain_hbm = f32[1,896]{1,0:T(1,128)} reshape(f32[896]{0:T(1024)} %param.11) | data formatting | bytes 7168 | tf_op jit(solution)/shard_map/reshape | solution.py:205
  1.9 48.1 %combine_norm_project.1 = (bf16[32,896]{1,0:T(8,128)(2,1)}, bf16[4,1536]{1,0:T(4,128)(2,1)}, bf16[4,576]{1,0:T(4,128)(2,1)}) custom-call(s32[8,32]{1,0:T(8,128)} %bitcast.3, f32[1,2,256]{2,1,0:T(2,128)} %gates_hbm.1, bf16[1,256,2,896]{3,2,1,0:T(2,128)(2,1)} %rows_hbm.1, bf16[32,896]{1,0:T(8,128)(2,1)} %res_hbm.1, f32[1,896]{1,0:T(1,128)} %reshape.9.gain_hbm, ...), custom_call_target="tpu_custom_call" | custom-call | tf_op jit(solution)/shard_map/combine_norm_project/pallas_call | solution.py:172
  50.0 1.4 %copy.13 = bf16[32,896]{1,0:T(8,128)(2,1)} copy(bf16[32,896]{1,0:T(8,128)(2,1)} %get-tuple-element.6) | data formatting | bytes 114688
  51.4 1.3 %copy.14 = bf16[4,1536]{1,0:T(4,128)(2,1)} copy(bf16[4,1536]{1,0:T(4,128)(2,1)} %get-tuple-element.7) | data formatting | bytes 24576
  52.7 1.3 %copy.15 = bf16[4,576]{1,0:T(4,128)(2,1)} copy(bf16[4,576]{1,0:T(4,128)(2,1)} %get-tuple-element.8) | data formatting | bytes 9216

commit v2 on v1

--- a/solution.py
+++ b/solution.py
@@ -23,10 +23,38 @@
 MESH = pl.DeviceIdType.MESH
 
 
-def partner(me, k):
-    dx, dy, dc = k & 7, (k + (k >> 3)) & 7, k >> 6
-    y, x, c = me >> 4, (me >> 1) & 7, me & 1
-    return (((y + dy) & 7) << 4) | (((x + dx) & 7) << 1) | ((c + dc) & 1)
+def hops(shift):
+    return min(shift, 8 - shift)
+
+
+SHIFTS = sorted(
+    ((y, x) for y in range(8) for x in range(8) if (y, x) != (0, 0)),
+    key=lambda shift: (-hops(shift[0]) - hops(shift[1]), (shift[0] * 3 + shift[1] * 5) % 8),
+)
+PER_WORD = 5
+WORDS = [
+    (
+        sum((8 * y + x) << (6 * place) for place, (y, x) in enumerate(SHIFTS[at : at + PER_WORD])),
+        len(SHIFTS[at : at + PER_WORD]),
+    )
+    for at in range(0, len(SHIFTS), PER_WORD)
+]
+RING = (4, 3, 5, 2, 6, 1, 7)
+
+
+def for_others(me, visit):
+    y, x = me >> 4, (me >> 1) & 7
+    for word, count in WORDS:
+
+        def step(place, carry, word=word):
+            shift = (jnp.int32(word) >> (6 * place)) & 63
+            chip = (((y + (shift >> 3)) & 7) << 4) | (((x + shift) & 7) << 1)
+            visit(chip | ((me + 1) & 1))
+            visit(chip | (me & 1))
+            return carry
+
+        lax.fori_loop(0, count, step, 0)
+    visit(me ^ 1)
 
 
 def wait_bytes(ref, sem):
@@ -55,14 +83,11 @@
 
     barrier = pltpu.get_barrier_semaphore()
 
-    def greet(k, carry):
-        pl.semaphore_signal(
-            barrier, inc=1, device_id={"node": partner(me, k)}, device_id_type=MESH
-        )
-        return carry
-
-    lax.fori_loop(1, NODES, greet, 0)
-    for k in range(1, LOCALS):
+    def greet(other):
+        pl.semaphore_signal(barrier, inc=1, device_id={"node": other}, device_id_type=MESH)
+
+    for_others(me, greet)
+    for k in RING:
         pl.semaphore_signal(barrier, inc=1, device_id={"local": (z + k) & 7}, device_id_type=MESH)
 
     loads[0].wait()
@@ -76,15 +101,13 @@
 
     pl.semaphore_wait(barrier, NODES - 1 + LOCALS - 1)
 
-    def push(k, carry):
-        other = partner(me, k)
+    def push(other):
         pltpu.make_async_remote_copy(
             src_ref=send.at[:, other], dst_ref=recv.at[:, me], send_sem=send_sem, recv_sem=recv_sem,
             device_id={"node": other}, device_id_type=MESH,
         ).start()
-        return carry
-
-    lax.fori_loop(1, NODES, push, 0)
+
+    for_others(me, push)
     pltpu.make_async_copy(send.at[:, me], recv.at[:, me], recv_sem).start()
 
     for load in loads[2:5]:
@@ -113,15 +136,29 @@
         hid_out[:, cols] = hidden
         hidden = hidden.astype(f32)
         squares = squares + hidden * hidden
-        scaled[:, cols] = (hidden * gain[:, cols]).astype(bf16)
+        scaled[:, cols] = (hidden * gain[cols][None, :]).astype(bf16)
 
     loads[5].wait()
+    zsend_rows = zsend.reshape(LAT_BLOCKS, TOK, 128)
+
+    def pass_on(blocks):
+        for k in RING:
+            other = (z + k) & 7
+            pltpu.make_async_remote_copy(
+                src_ref=zsend.at[blocks, other], dst_ref=zrecv.at[z, blocks], send_sem=zsend_sem,
+                recv_sem=zrecv_sem, device_id={"local": other}, device_id_type=MESH,
+            ).start()
+        pltpu.make_async_copy(zsend.at[blocks, z], zrecv.at[z, blocks], zrecv_sem).start()
+
+    stream = scaled[...]
+    query = jnp.dot(stream, wq[:, 0:1024], preferred_element_type=f32)
+    for block in range(8):
+        zsend_rows[block] = query[:, 128 * block : 128 * block + 128].astype(bf16)
+    pass_on(pl.ds(0, 8))
+    query = jnp.dot(stream, wq[:, 1024:QL], preferred_element_type=f32)
+    for block in range(4):
+        zsend_rows[8 + block] = query[:, 128 * block : 128 * block + 128].astype(bf16)
     loads[6].wait()
-    zsend_rows = zsend.reshape(LAT_BLOCKS, TOK, 128)
-    stream = scaled[...]
-    query = jnp.dot(stream, wq[...], preferred_element_type=f32)
-    for block in range(12):
-        zsend_rows[block] = query[:, 128 * block : 128 * block + 128].astype(bf16)
     keys = lax.dot_general(stream, wkv[...], (((1,), (1,)), ((), ())), preferred_element_type=f32)
     for block in range(4):
         zsend_rows[12 + block] = keys[:, 128 * block : 128 * block + 128].astype(bf16)
@@ -136,13 +173,7 @@
         ],
         axis=1,
     )
-    for k in range(1, LOCALS):
-        other = (z + k) & 7
-        pltpu.make_async_remote_copy(
-            src_ref=zsend.at[:, other], dst_ref=zrecv.at[z], send_sem=zsend_sem, recv_sem=zrecv_sem,
-            device_id={"local": other}, device_id_type=MESH,
-        ).start()
-    pltpu.make_async_copy(zsend.at[:, z], zrecv.at[z], zrecv_sem).start()
+    pass_on(pl.ds(8, 9))
     wait_bytes(send.at[:, pl.ds(0, NODES - 1)], send_sem)
     wait_bytes(zrecv, zrecv_sem)
 
@@ -166,16 +197,24 @@
     wait_bytes(zrecv.at[pl.ds(0, LOCALS - 1)], zsend_sem)
 
 
+def write_out(hidden, query, keys, hid_out, q_out, kv_out, sem):
+    copies = [
+        pltpu.make_async_copy(source, target, sem.at[i])
+        for i, (source, target) in enumerate([(hidden, hid_out), (query, q_out), (keys, kv_out)])
+    ]
+    for copy in copies:
+        copy.start()
+    for copy in copies:
+        copy.wait()
+
+
 def on_device(expert_ids, slot_gates, expert_rows, residual, norm_gain, w_q_down, w_kv_down):
     anywhere = pl.BlockSpec(memory_space=pl.ANY)
     vmem = pl.BlockSpec(memory_space=pltpu.VMEM)
-    return pl.pallas_call(
+    shapes = ((TOK, COLS), (OWN, QL), (OWN, KVL))
+    results = pl.pallas_call(
         kernel,
-        out_shape=(
-            jax.ShapeDtypeStruct((TOK, COLS), bf16),
-            jax.ShapeDtypeStruct((OWN, QL), bf16),
-            jax.ShapeDtypeStruct((OWN, KVL), bf16),
-        ),
+        out_shape=tuple(pltpu.VMEM(shape, bf16) for shape in shapes),
         in_specs=[anywhere] * 7,
         out_specs=(vmem,) * 3,
         scratch_shapes=[
@@ -183,7 +222,7 @@
             pltpu.VMEM((2, SLOTS), f32),
             pltpu.VMEM((SLOTS, 2, COLS), bf16),
             pltpu.VMEM((TOK, COLS), bf16),
-            pltpu.VMEM((1, COLS), f32),
+            pltpu.VMEM((COLS,), f32),
             pltpu.VMEM((COLS, QL), bf16),
             pltpu.VMEM((KVL, COLS), bf16),
             pltpu.VMEM((BLOCKS, NODES, 2, 128), bf16),
@@ -202,9 +241,17 @@
         ),
         name="combine_norm_project",
     )(
-        expert_ids.T, slot_gates, expert_rows, residual, norm_gain.reshape(1, COLS), w_q_down,
+        expert_ids.T, slot_gates, expert_rows, residual, norm_gain, w_q_down,
         w_kv_down.T,
     )
+    return pl.pallas_call(
+        write_out,
+        out_shape=tuple(jax.ShapeDtypeStruct(shape, bf16) for shape in shapes),
+        in_specs=[vmem] * 3,
+        out_specs=(anywhere,) * 3,
+        scratch_shapes=[pltpu.SemaphoreType.DMA((3,))],
+        name="write_out",
+    )(*results)
 
 
 def solution(mesh):

time: 54.3 us -> 48.7 us (0.90)
  local copies, waits for them, and re-layouts: 5.31 us -> 1.8 us
  Pallas kernels: 48.1 us -> 46 us
    unnamed x3 -> x6, local copies, waits for them, and re-layouts: 4.04 us -> 1.8 us
    pallas_call x1 -> x2, Pallas kernels: 48.1 us -> 46 us  [the longest x1 44.6 us: on_device(): pl.pallas_call(kernel, out_shape=tuple((pltpu.VMEM(shape, bf16) for shape...]
    reshape x1 -> x0, local copies, waits for them, and re-layouts: 1.27 us -> none  [on_device(): norm_gain.reshape(1, COLS)]
where the time goes in v2:
time: 48.7 us; the launch traced here: 48.5 us
  Pallas kernels  46 us (94%)
  local copies, waits for them, and re-layouts  1.8 us (4%)
  between operations  0.65 us (1%)
    pallas_call x1, Pallas kernels, on_device(): pl.pallas_call(kernel, out_shape=tuple((pltpu.VMEM(shape, bf16) for shape...  44.6 us
    unnamed x6, local copies, waits for them, and re-layouts  1.8 us
    pallas_call x1, Pallas kernels, on_device(): pl.pallas_call(write_out, out_shape=tuple((jax.ShapeDtypeStruct(shape, bf...  1.49 us

profile of v2, /device:TPU:1, one launch (start us, length us, event | category | flops | bytes accessed | tf_op | source)
XLA Modules:
  0.0 48.5 jit_solution(7053747677922302582)
XLA Ops:
  0.6 44.6 %combine_norm_project.1 = (bf16[32,896]{1,0:T(8,128)(2,1)S(1)}, bf16[4,1536]{1,0:T(4,128)(2,1)S(1)}, bf16[4,576]{1,0:T(4,128)(2,1)S(1)}) custom-call(s32[8,32]{1,0:T(8,128)} %bitcast.3, f32[1,2,256]{2,1,0:T(2,128)} %gates_hbm.1, bf16[1,256,2,896]{3,2,1,0:T(2,128)(2,1)} %rows_hbm.1, bf16[32,896]{1,0:T(8,128)(2,1)} %res_hbm.1, f32[896]{0:T(1024)} %gain_hbm.1, ...), custom_call_target="tpu_custom_call" | custom-call | tf_op jit(solution)/shard_map/combine_norm_project/pallas_call | solution.py:215
  45.2 0.0 copy-start
  45.2 0.6 %copy-done = bf16[32,896]{1,0:T(8,128)(2,1)} copy-done((bf16[32,896]{1,0:T(8,128)(2,1)}, bf16[32,896]{1,0:T(8,128)(2,1)S(1)}, u32[]{:S(2)}) %copy-start) | copy-done | bytes 57368
  45.8 0.0 copy-start.1
  45.8 0.6 %copy-done.1 = bf16[4,1536]{1,0:T(4,128)(2,1)} copy-done((bf16[4,1536]{1,0:T(4,128)(2,1)}, bf16[4,1536]{1,0:T(4,128)(2,1)S(1)}, u32[]{:S(2)}) %copy-start.1) | copy-done | bytes 12312
  46.4 0.0 copy-start.2
  46.4 0.6 %copy-done.2 = bf16[4,576]{1,0:T(4,128)(2,1)} copy-done((bf16[4,576]{1,0:T(4,128)(2,1)}, bf16[4,576]{1,0:T(4,128)(2,1)S(1)}, u32[]{:S(2)}) %copy-start.2) | copy-done | bytes 4632
  47.0 1.5 %write_out.1 = (bf16[32,896]{1,0:T(8,128)(2,1)}, bf16[4,1536]{1,0:T(4,128)(2,1)}, bf16[4,576]{1,0:T(4,128)(2,1)}) custom-call(bf16[32,896]{1,0:T(8,128)(2,1)} %copy-done, bf16[4,1536]{1,0:T(4,128)(2,1)} %copy-done.1, bf16[4,576]{1,0:T(4,128)(2,1)} %copy-done.2), custom_call_target="tpu_custom_call" | custom-call | tf_op jit(solution)/shard_map/write_out/pallas_call | solution.py:247
Async XLA Ops:
  45.2 0.6 %copy-start = (bf16[32,896]{1,0:T(8,128)(2,1)}, bf16[32,896]{1,0:T(8,128)(2,1)S(1)}, u32[]{:S(2)}) copy-start(bf16[32,896]{1,0:T(8,128)(2,1)S(1)} %get-tuple-element.6.hidden) | copy-start | bytes 172036
  45.8 0.6 %copy-start.1 = (bf16[4,1536]{1,0:T(4,128)(2,1)}, bf16[4,1536]{1,0:T(4,128)(2,1)S(1)}, u32[]{:S(2)}) copy-start(bf16[4,1536]{1,0:T(4,128)(2,1)S(1)} %get-tuple-element.7.query) | copy-start | bytes 36868
  46.4 0.6 %copy-start.2 = (bf16[4,576]{1,0:T(4,128)(2,1)}, bf16[4,576]{1,0:T(4,128)(2,1)S(1)}, u32[]{:S(2)}) copy-start(bf16[4,576]{1,0:T(4,128)(2,1)S(1)} %get-tuple-element.8.keys) | copy-start | bytes 13828

commit v3 on v2

--- a/solution.py
+++ b/solution.py
@@ -39,7 +39,6 @@
     )
     for at in range(0, len(SHIFTS), PER_WORD)
 ]
-RING = (4, 3, 5, 2, 6, 1, 7)
 
 
 def for_others(me, visit):
@@ -65,7 +64,7 @@
     ids_hbm, gates_hbm, rows_hbm, res_hbm, gain_hbm, wq_hbm, wkv_hbm,
     hid_out, q_out, kv_out,
     ids, gates, rows, res, gain, wq, wkv, send, recv, scaled, zsend, zrecv,
-    in_sem, send_sem, recv_sem, zsend_sem, zrecv_sem,
+    in_sem, above_sem, send_sem, recv_sem, zsend_sem, zrecv_sem,
 ):
     me = lax.axis_index("node")
     z = lax.axis_index("local")
@@ -87,8 +86,11 @@
         pl.semaphore_signal(barrier, inc=1, device_id={"node": other}, device_id_type=MESH)
 
     for_others(me, greet)
-    for k in RING:
-        pl.semaphore_signal(barrier, inc=1, device_id={"local": (z + k) & 7}, device_id_type=MESH)
+    for k in range(1, LOCALS):
+
+        @pl.when(z + k < LOCALS)
+        def _():
+            pl.semaphore_signal(barrier, inc=1, device_id={"local": z + k}, device_id_type=MESH)
 
     loads[0].wait()
     gate_columns = jnp.concatenate([gates[...], jnp.zeros((6, SLOTS), f32)], axis=0).T
@@ -99,7 +101,12 @@
     for block in range(BLOCKS):
         send_rows[block] = weighted[:, 128 * block : 128 * block + 128].astype(bf16)
 
-    pl.semaphore_wait(barrier, NODES - 1 + LOCALS - 1)
+    pl.semaphore_wait(barrier, NODES - 1 + z)
+    for k in range(1, LOCALS):
+
+        @pl.when(z >= k)
+        def _():
+            pl.semaphore_signal(above_sem, inc=1, device_id={"local": z - k}, device_id_type=MESH)
 
     def push(other):
         pltpu.make_async_remote_copy(
@@ -142,13 +149,18 @@
     zsend_rows = zsend.reshape(LAT_BLOCKS, TOK, 128)
 
     def pass_on(blocks):
-        for k in RING:
-            other = (z + k) & 7
+        for place in range(LOCALS - 1):
+            other = place + (place >= z).astype(jnp.int32)
             pltpu.make_async_remote_copy(
                 src_ref=zsend.at[blocks, other], dst_ref=zrecv.at[z, blocks], send_sem=zsend_sem,
                 recv_sem=zrecv_sem, device_id={"local": other}, device_id_type=MESH,
             ).start()
         pltpu.make_async_copy(zsend.at[blocks, z], zrecv.at[z, blocks], zrecv_sem).start()
+
+
+    @pl.when(z < LOCALS - 1)
+    def _():
+        pl.semaphore_wait(above_sem, LOCALS - 1 - z)
 
     stream = scaled[...]
     query = jnp.dot(stream, wq[:, 0:1024], preferred_element_type=f32)
@@ -231,6 +243,7 @@
             pltpu.VMEM((LAT_BLOCKS, LOCALS, OWN, 128), bf16),
             pltpu.VMEM((LOCALS, LAT_BLOCKS, OWN, 128), bf16),
             pltpu.SemaphoreType.DMA((7,)),
+            pltpu.SemaphoreType.REGULAR,
             pltpu.SemaphoreType.DMA,
             pltpu.SemaphoreType.DMA,
             pltpu.SemaphoreType.DMA,
@@ -244,12 +257,14 @@
         expert_ids.T, slot_gates, expert_rows, residual, norm_gain, w_q_down,
         w_kv_down.T,
     )
+    results = [pltpu.with_memory_space_constraint(result, pltpu.VMEM) for result in results]
     return pl.pallas_call(
         write_out,
         out_shape=tuple(jax.ShapeDtypeStruct(shape, bf16) for shape in shapes),
         in_specs=[vmem] * 3,
         out_specs=(anywhere,) * 3,
         scratch_shapes=[pltpu.SemaphoreType.DMA((3,))],
+        compiler_params=pltpu.CompilerParams(vmem_limit_bytes=1024 * 1024),
         name="write_out",
     )(*results)
 

time: 48.7 us -> 45.5 us (0.934)
  local copies, waits for them, and re-layouts: 1.8 us -> 0 us
  Pallas kernels: 46 us -> 44.7 us
    unnamed x6 -> x0, local copies, waits for them, and re-layouts: 1.8 us -> none
    pallas_call x1, Pallas kernels: 1.49 us -> 0.66 us  [on_device(): pl.pallas_call(write_out, out_shape=tuple((jax.ShapeDtypeStruct(shape, bf...]
    pallas_call x1, Pallas kernels: 44.6 us -> 44 us  [on_device(): pl.pallas_call(kernel, out_shape=tuple((pltpu.VMEM(shape, bf16) for shape...]
where the time goes in v3:
time: 45.5 us; the launch traced here: 45.3 us
  Pallas kernels  44.7 us (98%)
  between operations  0.64 us (1%)
    pallas_call x1, Pallas kernels, on_device(): pl.pallas_call(kernel, out_shape=tuple((pltpu.VMEM(shape, bf16) for shape...  44 us

profile of v3, /device:TPU:1, one launch (start us, length us, event | category | flops | bytes accessed | tf_op | source)
XLA Modules:
  0.0 45.3 jit_solution(17328474666248079678)
XLA Ops:
  0.6 44.0 %combine_norm_project.1 = (bf16[32,896]{1,0:T(8,128)(2,1)S(1)}, bf16[4,1536]{1,0:T(4,128)(2,1)S(1)}, bf16[4,576]{1,0:T(4,128)(2,1)S(1)}) custom-call(s32[8,32]{1,0:T(8,128)} %bitcast.3, f32[1,2,256]{2,1,0:T(2,128)} %gates_hbm.1, bf16[1,256,2,896]{3,2,1,0:T(2,128)(2,1)} %rows_hbm.1, bf16[32,896]{1,0:T(8,128)(2,1)} %res_hbm.1, f32[896]{0:T(1024)} %gain_hbm.1, ...), custom_call_target="tpu_custom_call" | custom-call | tf_op jit(solution)/shard_map/combine_norm_project/pallas_call | solution.py:227
  44.7 0.7 %write_out.1 = (bf16[32,896]{1,0:T(8,128)(2,1)}, bf16[4,1536]{1,0:T(4,128)(2,1)}, bf16[4,576]{1,0:T(4,128)(2,1)}) custom-call(bf16[32,896]{1,0:T(8,128)(2,1)S(1)} %get-tuple-element.6.hidden, bf16[4,1536]{1,0:T(4,128)(2,1)S(1)} %get-tuple-element.7.query, bf16[4,576]{1,0:T(4,128)(2,1)S(1)} %get-tuple-element.8.keys), custom_call_target="tpu_custom_call" | custom-call | tf_op jit(solution)/shard_map/write_out/pallas_call | solution.py:261

commit v4 on v3

--- a/solution.py
+++ b/solution.py
@@ -27,33 +27,34 @@
     return min(shift, 8 - shift)
 
 
-SHIFTS = sorted(
+FIRST = 32
+
+
+def turned(shift):
+    turns = []
+    for _ in range(4):
+        if shift not in turns:
+            turns.append(shift)
+        shift = (shift[1], -shift[0] % 8)
+    return turns
+
+
+SHIFTS = []
+for first in sorted(
     ((y, x) for y in range(8) for x in range(8) if (y, x) != (0, 0)),
-    key=lambda shift: (-hops(shift[0]) - hops(shift[1]), (shift[0] * 3 + shift[1] * 5) % 8),
-)
-PER_WORD = 5
-WORDS = [
-    (
-        sum((8 * y + x) << (6 * place) for place, (y, x) in enumerate(SHIFTS[at : at + PER_WORD])),
-        len(SHIFTS[at : at + PER_WORD]),
-    )
-    for at in range(0, len(SHIFTS), PER_WORD)
-]
-
-
-def for_others(me, visit):
-    y, x = me >> 4, (me >> 1) & 7
-    for word, count in WORDS:
-
-        def step(place, carry, word=word):
-            shift = (jnp.int32(word) >> (6 * place)) & 63
-            chip = (((y + (shift >> 3)) & 7) << 4) | (((x + shift) & 7) << 1)
-            visit(chip | ((me + 1) & 1))
-            visit(chip | (me & 1))
-            return carry
-
-        lax.fori_loop(0, count, step, 0)
-    visit(me ^ 1)
+    key=lambda shift: (-hops(shift[0]) - hops(shift[1]), abs(hops(shift[0]) - hops(shift[1])), shift),
+):
+    SHIFTS += [shift for shift in turned(first) if shift not in SHIFTS]
+
+
+def for_others(me, visit, shifts=SHIFTS, own_chip=True):
+    y, x, core = me >> 4, (me >> 1) & 7, me & 1
+    for shift_y, shift_x in shifts:
+        chip = (((y + shift_y) & 7) << 4) | (((x + shift_x) & 7) << 1)
+        visit(chip | (1 - core))
+        visit(chip | core)
+    if own_chip:
+        visit(me ^ 1)
 
 
 def wait_bytes(ref, sem):
@@ -77,7 +78,7 @@
             ]
         )
     ]
-    for load in loads:
+    for load in loads[:2]:
         load.start()
 
     barrier = pltpu.get_barrier_semaphore()
@@ -91,6 +92,9 @@
         @pl.when(z + k < LOCALS)
         def _():
             pl.semaphore_signal(barrier, inc=1, device_id={"local": z + k}, device_id_type=MESH)
+
+    for load in loads[2:]:
+        load.start()
 
     loads[0].wait()
     gate_columns = jnp.concatenate([gates[...], jnp.zeros((6, SLOTS), f32)], axis=0).T
@@ -102,11 +106,6 @@
         send_rows[block] = weighted[:, 128 * block : 128 * block + 128].astype(bf16)
 
     pl.semaphore_wait(barrier, NODES - 1 + z)
-    for k in range(1, LOCALS):
-
-        @pl.when(z >= k)
-        def _():
-            pl.semaphore_signal(above_sem, inc=1, device_id={"local": z - k}, device_id_type=MESH)
 
     def push(other):
         pltpu.make_async_remote_copy(
@@ -114,31 +113,36 @@
             device_id={"node": other}, device_id_type=MESH,
         ).start()
 
-    for_others(me, push)
+    for_others(me, push, SHIFTS[:FIRST], own_chip=False)
+    for k in range(1, LOCALS):
+
+        @pl.when(z >= k)
+        def _():
+            pl.semaphore_signal(above_sem, inc=1, device_id={"local": z - k}, device_id_type=MESH)
+
+    for_others(me, push, SHIFTS[FIRST:])
     pltpu.make_async_copy(send.at[:, me], recv.at[:, me], recv_sem).start()
 
     for load in loads[2:5]:
         load.wait()
-    slot = lax.broadcasted_iota(jnp.int32, (SLOTS, TOK), 0)
-    nodes = ids[...] >> 1
+    slot = lax.broadcasted_iota(jnp.int32, (SLOTS, 128), 0)
+    nodes = jnp.concatenate([ids[...] >> 1, jnp.zeros((8, 128 - TOK), jnp.int32)], axis=1)
     routed = nodes[0:1, :] == (slot >> 1)
     for entry in range(1, 8):
         routed = routed | (nodes[entry : entry + 1, :] == (slot >> 1))
     earlier = (
-        lax.broadcasted_iota(jnp.int32, (TOK, TOK), 0)
-        < lax.broadcasted_iota(jnp.int32, (TOK, TOK), 1)
+        lax.broadcasted_iota(jnp.int32, (128, 128), 0)
+        < lax.broadcasted_iota(jnp.int32, (128, 128), 1)
     ).astype(bf16)
     rank = jnp.dot(routed.astype(bf16), earlier, preferred_element_type=f32)
-    serves = (routed & (rank == (slot & 1).astype(f32))).astype(bf16)
+    serves = (routed & (rank == (slot & 1).astype(f32))).astype(f32).T[0:TOK].astype(bf16)
 
     wait_bytes(recv, recv_sem)
     recv_rows = recv.reshape(BLOCKS, SLOTS, 128)
     squares = jnp.zeros((TOK, 128), f32)
     for block in range(BLOCKS):
         cols = slice(128 * block, 128 * block + 128)
-        combined = lax.dot_general(
-            serves, recv_rows[block], (((0,), (0,)), ((), ())), preferred_element_type=f32
-        )
+        combined = jnp.dot(serves, recv_rows[block], preferred_element_type=f32)
         hidden = (res[:, cols].astype(f32) + combined).astype(bf16)
         hid_out[:, cols] = hidden
         hidden = hidden.astype(f32)

time: 45.5 us -> 45.4 us (level)
  no operation moved by 1% of the time
where the time goes in v4:
time: 45.4 us; the launch traced here: 45.2 us
  Pallas kernels  44.6 us (98%)
  between operations  0.64 us (1%)
    pallas_call x1, Pallas kernels, on_device(): pl.pallas_call(kernel, out_shape=tuple((pltpu.VMEM(shape, bf16) for shape...  43.9 us

profile of v4, /device:TPU:1, one launch (start us, length us, event | category | flops | bytes accessed | tf_op | source)
XLA Modules:
  0.0 45.2 jit_solution(2381834542401325766)
XLA Ops:
  0.6 43.9 %combine_norm_project.1 = (bf16[32,896]{1,0:T(8,128)(2,1)S(1)}, bf16[4,1536]{1,0:T(4,128)(2,1)S(1)}, bf16[4,576]{1,0:T(4,128)(2,1)S(1)}) custom-call(s32[8,32]{1,0:T(8,128)} %bitcast.3, f32[1,2,256]{2,1,0:T(2,128)} %gates_hbm.1, bf16[1,256,2,896]{3,2,1,0:T(2,128)(2,1)} %rows_hbm.1, bf16[32,896]{1,0:T(8,128)(2,1)} %res_hbm.1, f32[896]{0:T(1024)} %gain_hbm.1, ...), custom_call_target="tpu_custom_call" | custom-call | tf_op jit(solution)/shard_map/combine_norm_project/pallas_call | solution.py:231
  44.6 0.7 %write_out.1 = (bf16[32,896]{1,0:T(8,128)(2,1)}, bf16[4,1536]{1,0:T(4,128)(2,1)}, bf16[4,576]{1,0:T(4,128)(2,1)}) custom-call(bf16[32,896]{1,0:T(8,128)(2,1)S(1)} %get-tuple-element.6.hidden, bf16[4,1536]{1,0:T(4,128)(2,1)S(1)} %get-tuple-element.7.query, bf16[4,576]{1,0:T(4,128)(2,1)S(1)} %get-tuple-element.8.keys), custom_call_target="tpu_custom_call" | custom-call | tf_op jit(solution)/shard_map/write_out/pallas_call | solution.py:265

commit v5 on v4

--- a/solution.py
+++ b/solution.py
@@ -157,9 +157,9 @@
             other = place + (place >= z).astype(jnp.int32)
             pltpu.make_async_remote_copy(
                 src_ref=zsend.at[blocks, other], dst_ref=zrecv.at[z, blocks], send_sem=zsend_sem,
-                recv_sem=zrecv_sem, device_id={"local": other}, device_id_type=MESH,
+                recv_sem=zrecv_sem.at[z], device_id={"local": other}, device_id_type=MESH,
             ).start()
-        pltpu.make_async_copy(zsend.at[blocks, z], zrecv.at[z, blocks], zrecv_sem).start()
+        pltpu.make_async_copy(zsend.at[blocks, z], zrecv.at[z, blocks], zrecv_sem.at[z]).start()
 
 
     @pl.when(z < LOCALS - 1)
@@ -191,11 +191,11 @@
     )
     pass_on(pl.ds(8, 9))
     wait_bytes(send.at[:, pl.ds(0, NODES - 1)], send_sem)
-    wait_bytes(zrecv, zrecv_sem)
 
     zrecv_rows = zrecv.reshape(LOCALS, LAT_BLOCKS * OWN, 128)
-    total = zrecv_rows[0].astype(f32)
-    for source in range(1, LOCALS):
+    total = jnp.zeros((LAT_BLOCKS * OWN, 128), f32)
+    for source in range(LOCALS):
+        wait_bytes(zrecv.at[source], zrecv_sem.at[source])
         total = total + zrecv_rows[source].astype(f32)
     last = total[16 * OWN : 17 * OWN]
     square_sum = (last[:, HI_LANE : HI_LANE + 1] + last[:, LO_LANE : LO_LANE + 1]) * 4.0
@@ -251,7 +251,7 @@
             pltpu.SemaphoreType.DMA,
             pltpu.SemaphoreType.DMA,
             pltpu.SemaphoreType.DMA,
-            pltpu.SemaphoreType.DMA,
+            pltpu.SemaphoreType.DMA((LOCALS,)),
         ],
         compiler_params=pltpu.CompilerParams(
             collective_id=0, has_side_effects=True, vmem_limit_bytes=56 * 1024 * 1024

time: 45.4 us -> 45.4 us (level)
  no operation moved by 1% of the time
where the time goes in v5:
time: 45.4 us; the launch traced here: 45.3 us
  Pallas kernels  44.6 us (98%)
  between operations  0.64 us (1%)
    pallas_call x1, Pallas kernels, on_device(): pl.pallas_call(kernel, out_shape=tuple((pltpu.VMEM(shape, bf16) for shape...  44 us

profile of v5, /device:TPU:1, one launch (start us, length us, event | category | flops | bytes accessed | tf_op | source)
XLA Modules:
  0.0 45.3 jit_solution(11050513441142420203)
XLA Ops:
  0.6 44.0 %combine_norm_project.1 = (bf16[32,896]{1,0:T(8,128)(2,1)S(1)}, bf16[4,1536]{1,0:T(4,128)(2,1)S(1)}, bf16[4,576]{1,0:T(4,128)(2,1)S(1)}) custom-call(s32[8,32]{1,0:T(8,128)} %bitcast.3, f32[1,2,256]{2,1,0:T(2,128)} %gates_hbm.1, bf16[1,256,2,896]{3,2,1,0:T(2,128)(2,1)} %rows_hbm.1, bf16[32,896]{1,0:T(8,128)(2,1)} %res_hbm.1, f32[896]{0:T(1024)} %gain_hbm.1, ...), custom_call_target="tpu_custom_call" | custom-call | tf_op jit(solution)/shard_map/combine_norm_project/pallas_call | solution.py:231
  44.6 0.7 %write_out.1 = (bf16[32,896]{1,0:T(8,128)(2,1)}, bf16[4,1536]{1,0:T(4,128)(2,1)}, bf16[4,576]{1,0:T(4,128)(2,1)}) custom-call(bf16[32,896]{1,0:T(8,128)(2,1)S(1)} %get-tuple-element.6.hidden, bf16[4,1536]{1,0:T(4,128)(2,1)S(1)} %get-tuple-element.7.query, bf16[4,576]{1,0:T(4,128)(2,1)S(1)} %get-tuple-element.8.keys), custom_call_target="tpu_custom_call" | custom-call | tf_op jit(solution)/shard_map/write_out/pallas_call | solution.py:265
